TPU v7x, 128 devices: a whole 4x4x4 slice. The times are simulated.
128 devices in a mesh: dp: 16 (over x, z), tensor: 8 (over y, core).
Axes of the slice: x: 4, y: 4, z: 4, core: 2. Of those that a mesh axis runs over, the one named last changes fastest.
Arguments:
- tokens: bfloat16 [16384, 2880], P(('dp', 'tensor'))
- positions: int32 [16, 1024], P('dp'), may hold values from 0 to 32767, as said below
- doc_ids: int32 [16, 1024], P('dp'), may hold values from 0 to 3, never falling along the last dimension, each value on 1 to 512 neighbouring positions
- w_query: bfloat16 [2880, 4096], P('dp', 'tensor')
- key_weight: bfloat16 [2880, 512], P('dp', 'tensor')
- value_weight: bfloat16 [2880, 512], P('dp', 'tensor'), may hold values from -0.109375 to 0.109375
- w_out: bfloat16 [4096, 2880], P('tensor', 'dp'), may hold values from -0.375 to 0.375
- attn_gain: float32 [2880], replicated, may hold values from 0.25 to 1.75
- moe_gain: float32 [2880], replicated, may hold values from 0.25 to 1.75
- expert_ids: int32 [16384, 4], P(('dp', 'tensor')), may hold values from 0 to 127, all different within a row; in each aligned block of 128 rows (0 to 127, 128 to 255, ...) at most 6 rows name the same one
- gate_weights: float32 [16384, 4], P(('dp', 'tensor')), may hold values from 0.1 to 1
- w_gate_up: bfloat16 [128, 2880, 2880], P(('dp', 'tensor')), may hold values from -0.109375 to 0.109375
- w_down: bfloat16 [128, 1440, 2880], P(('dp', 'tensor')), may hold values from -0.15625 to 0.15625
Outputs:
- mixed: bfloat16 [16384, 2880], P(('dp', 'tensor'))
Inputs may be any that keep to these rules, and one draw needn't show every extreme that they name: Within a window the positions rise by one from 0, except for one jump forward at a point drawn per window; in some window the last position is 32767. `expert_ids`: A token names 4 different experts. In each aligned block of 128 rows (the rows of one device) no expert is named by more than 6 rows.
All inputs are finite; a program needn't handle non-finite values.
Results may differ from a plain program's by a relative error of at most 0.02.
The roundings to bfloat16 on the way count: a program that leaves them out, or rounds other values in their place, can miss the bound.
Values may be sent and summed in bfloat16 or wider, within the bound.
No kernel may reach another device: no remote copies, remote signals or barrier semaphores. Data moves between devices by JAX's collectives and lax.ppermute only.
A program may use at most 128 MiB of HBM per device.

v0:
```python
import math

import jax
import jax.numpy as jnp
from jax import lax
from jax.sharding import PartitionSpec as P

HEAD_SIZE = 64


def rms_norm(value_rows, gain):
    mean_square = jnp.mean(value_rows * value_rows, axis=-1, keepdims=True)
    return value_rows * lax.rsqrt(mean_square + 1e-05) * gain


def rotate(value_rows, position):
    half = value_rows.shape[-1] // 2
    freq = jnp.exp(
        jnp.arange(half, dtype=jnp.float32) * (-2.0 * math.log(150000.0) / value_rows.shape[-1])
    )
    angle = position.astype(jnp.float32)[:, None] * freq[None, :]
    cosine = jnp.cos(angle)[:, None, :]
    sine = jnp.sin(angle)[:, None, :]
    first = value_rows[..., :half]
    second = value_rows[..., half:]
    return jnp.concatenate(
        [first * cosine - second * sine, second * cosine + first * sine], axis=-1
    )


def expert_apply(received, gate_up, down):
    sources, slots, width = received.shape
    token_rows = received.reshape(sources * slots, width)
    both = jnp.dot(token_rows, gate_up, preferred_element_type=jnp.float32)
    hidden = both.shape[1] // 2
    gate = both[:, :hidden]
    up = both[:, hidden:]
    act = (gate * jax.nn.sigmoid(1.702 * gate) * (up + 1.0)).astype(jnp.bfloat16)
    result = jnp.dot(act, down, preferred_element_type=jnp.float32).astype(jnp.bfloat16)
    return result.reshape(sources, slots, width)


def body(
    tokens,
    positions,
    doc_ids,
    w_query,
    key_weight,
    value_weight,
    w_out,
    attn_gain,
    moe_gain,
    expert_ids,
    gate_weights,
    w_gate_up,
    w_down,
):
    resid_in = tokens.astype(jnp.float32)
    normed = rms_norm(resid_in, attn_gain).astype(jnp.bfloat16)
    full_query, full_key, full_value, full_out = (
        lax.all_gather(w_query, "dp", axis=0, tiled=True),
        lax.all_gather(key_weight, "dp", axis=0, tiled=True),
        lax.all_gather(value_weight, "dp", axis=0, tiled=True),
        lax.all_gather(w_out, "dp", axis=1, tiled=True),
    )
    joined = jnp.concatenate([full_query, full_key, full_value], axis=1)
    projected = jnp.dot(
        lax.all_gather(normed, "tensor", axis=0, tiled=True),
        joined,
        preferred_element_type=jnp.float32,
    )
    length = projected.shape[0]
    width_query = full_query.shape[1]
    width_key = full_key.shape[1]
    local_heads = width_query // HEAD_SIZE
    local_kv = width_key // HEAD_SIZE
    head_group = local_heads // local_kv
    position = positions[0]
    docs = doc_ids[0]
    query_rows = rotate(
        projected[:, :width_query].reshape(length, local_heads, HEAD_SIZE), position
    ).astype(jnp.bfloat16)
    key_rows = rotate(
        projected[:, width_query : width_query + width_key].reshape(length, local_kv, HEAD_SIZE),
        position,
    ).astype(jnp.bfloat16)
    value_rows = (
        projected[:, width_query + width_key :]
        .reshape(length, local_kv, HEAD_SIZE)
        .astype(jnp.bfloat16)
    )
    index = jnp.arange(length, dtype=jnp.int32)
    allowed = (index[:, None] >= index[None, :]) & (docs[:, None] == docs[None, :])
    grouped_heads = query_rows.reshape(length, local_kv, head_group, HEAD_SIZE).transpose(
        1, 2, 0, 3
    )

    def kv_head(parts):
        query_group, key_head, value_head = parts

        def one_query_head(query_head):
            scores = jnp.dot(
                query_head, key_head.T, preferred_element_type=jnp.float32
            ) * HEAD_SIZE ** (-0.5)
            masked = jnp.where(allowed, scores, -1e30)
            largest = jnp.max(masked, axis=-1, keepdims=True)
            weights = jnp.where(allowed, jnp.exp(masked - largest), 0.0)
            probs = (weights / jnp.sum(weights, axis=-1, keepdims=True)).astype(jnp.bfloat16)
            return jnp.dot(probs, value_head, preferred_element_type=jnp.float32).astype(
                jnp.bfloat16
            )

        return lax.map(one_query_head, query_group)

    mixed_heads = lax.map(
        kv_head, (grouped_heads, key_rows.transpose(1, 0, 2), value_rows.transpose(1, 0, 2))
    )
    heads = mixed_heads.transpose(2, 0, 1, 3).reshape(length, width_query)
    attn_out = lax.psum_scatter(
        jnp.dot(heads, full_out, preferred_element_type=jnp.float32).astype(jnp.bfloat16),
        "tensor",
        scatter_dimension=0,
        tiled=True,
    ).astype(jnp.float32)
    resid = resid_in + attn_out
    moe_in = rms_norm(resid, moe_gain).astype(jnp.bfloat16)
    rows_count, top = expert_ids.shape
    expert_count = lax.axis_size("dp") * lax.axis_size("tensor")
    capacity = max(2, rows_count * top * 3 // (2 * expert_count))
    flat_ids = expert_ids.reshape(-1)
    assigned = rows_count * top
    onehot = (flat_ids[:, None] == jnp.arange(expert_count, dtype=jnp.int32)[None, :]).astype(
        jnp.bfloat16
    )
    earlier = (jnp.arange(assigned)[:, None] > jnp.arange(assigned)[None, :]).astype(jnp.bfloat16)
    before = jnp.dot(earlier, onehot, preferred_element_type=jnp.float32)
    slot = jnp.sum(before * onehot.astype(jnp.float32), axis=-1).astype(jnp.int32)
    target = flat_ids * capacity + slot
    table = jnp.any(
        jnp.arange(expert_count * capacity, dtype=jnp.int32)[:, None, None]
        == target.reshape(rows_count, top)[None, :, :],
        axis=-1,
    ).astype(jnp.bfloat16)
    outgoing = jnp.dot(table, moe_in, preferred_element_type=jnp.float32).astype(jnp.bfloat16)
    outgoing = outgoing.reshape(expert_count, capacity, moe_in.shape[1])
    gate_up = w_gate_up[0]
    down = w_down[0]
    finished = expert_apply(
        lax.all_to_all(outgoing, ("dp", "tensor"), split_axis=0, concat_axis=0, tiled=True),
        gate_up,
        down,
    )
    returned = lax.all_to_all(finished, ("dp", "tensor"), split_axis=0, concat_axis=0, tiled=True)
    flat_back = returned.reshape(expert_count * capacity, moe_in.shape[1])
    picked = jnp.take(flat_back, target, axis=0).reshape(rows_count, top, moe_in.shape[1])
    share = gate_weights / jnp.sum(gate_weights, axis=-1, keepdims=True)
    moe_out = jnp.sum(picked.astype(jnp.float32) * share[:, :, None], axis=1)
    return (resid + moe_out).astype(jnp.bfloat16)


def solution(mesh):
    placed = (
        P(("dp", "tensor"), None),
        P("dp", None),
        P("dp", None),
        P("dp", "tensor"),
        P("dp", "tensor"),
        P("dp", "tensor"),
        P("tensor", "dp"),
        P(),
        P(),
        P(("dp", "tensor"), None),
        P(("dp", "tensor"), None),
        P(("dp", "tensor"), None, None),
        P(("dp", "tensor"), None, None),
    )
    return jax.shard_map(
        body, mesh=mesh, in_specs=placed, out_specs=P(("dp", "tensor"), None), check_vma=False
    )
```

profile of v0, /device:TPU:1, one launch (start us, length us, event | category | flops | bytes accessed | tf_op | source)
XLA Modules:
  0.0 547.1 jit_solution(9165569797998443567)
XLA Ops:
  9.8 1.8 fusion.39
  11.7 22.4 %all-gather.1 = bf16[16,180,64]{1,2,0:T(8,128)(2,1)S(1)} all-gather(bf16[1,180,64]{1,2,0:T(8,128)(2,1)S(1)} %bitcast.69), channel_id=1, replica_groups=mesh['dp'=16,'tensor'=8] {'dp'}, dimensions={0}, use_global_device_ids=true | all-gather | bytes 391680 | tf_op jit(solution)/shard_map/all_gather | solution.py:62
  34.7 19.9 %all-gather.2 = bf16[16,180,64]{1,2,0:T(8,128)(2,1)S(1)} all-gather(bf16[1,180,64]{1,2,0:T(8,128)(2,1)S(1)} %bitcast.70), channel_id=1, replica_groups=mesh['dp'=16,'tensor'=8] {'dp'}, dimensions={0}, use_global_device_ids=true | all-gather | bytes 391680 | tf_op jit(solution)/shard_map/all_gather | solution.py:63
  56.1 3.0 multiply_cosine_fusion
  59.0 2.7 all-gather.10.cloned.1.call-done
  61.8 4.3 reshape.273
  66.1 44.3 %all-gather.12.cloned.1.call-done = bf16[16,180,512]{2,1,0:T(8,128)(2,1)} async-done(((bf16[1,180,512]{2,1,0:T(8,128)(2,1)}), bf16[16,180,512]{2,1,0:T(8,128)(2,1)}) %all-gather.12.cloned.1.call-update) | async-done | bytes 2949136 | tf_op jit(solution)/shard_map/all_gather | solution.py:64
  110.4 4.3 reshape.279
  114.7 36.8 %all-gather.8.cloned.1.call-done = bf16[1024,2880]{1,0:T(8,128)(2,1)} async-done(((bf16[128,2880]{1,0:T(8,128)(2,1)}), bf16[1024,2880]{1,0:T(8,128)(2,1)}) %all-gather.8.cloned.1.call-update) | async-done | bytes 5898256 | tf_op jit(solution)/shard_map/all_gather | solution.py:68
  151.5 8.0 %fusion.25 = f32[1024,640]{0,1:T(8,128)S(1)} fusion(bf16[1024,2880]{1,0:T(8,128)(2,1)} %all-gather.8.cloned.1.call-done, bf16[2880,64]{1,0:T(8,128)(2,1)S(1)} %copy-done.3, bf16[2880,64]{1,0:T(8,128)(2,1)S(1)} %reshape.280, bf16[2880,512]{1,0:T(8,128)(2,1)} %reshape.273), kind=kOutput, calls=%fused_computation.33 | convolution fusion | flops 3785932800 | bytes 12206080 | tf_op jit(solution)/shard_map/dot_general | solution.py:67
  160.6 2.7 copy.92
  163.3 2.6 copy.93
  168.2 4.6 fusion.34
  174.0 37.2 %while.18 = (s32[]{:T(128)}, bf16[8,1024,64]{1,2,0:T(8,128)(2,1)}, bf16[8,1024,64]{2,1,0:T(8,128)(2,1)S(1)}, bf16[1024,64]{1,0:T(8,128)(2,1)S(1)}, bf16[1024,64]...) while((s32[]{:T(128)}, bf16[8,1024,64]{1,2,0:T(8,128)(2,1)}, ...), condition=%wide.region_4.5_spmd.clone, body=%wide.region_1.4_spmd.clone.sunk | while | flops 292616192 | bytes 13541969 | solution.py:113
  175.4 1.8 fusion.76
  177.2 1.9 fusion.77
  180.0 1.8 fusion.76
  181.8 1.9 fusion.77
  184.6 1.8 fusion.76
  186.4 1.9 fusion.77
  189.1 1.8 fusion.76
  191.0 1.9 fusion.77
  193.7 1.8 fusion.76
  195.6 1.9 fusion.77
  198.3 1.8 fusion.76
  200.2 1.9 fusion.77
  202.9 1.8 fusion.76
  204.8 1.9 fusion.77
  207.5 1.8 fusion.76
  209.3 1.9 fusion.77
  211.2 7.9 %convolution_convert_fusion = bf16[1024,2880]{0,1:T(8,128)(2,1)} fusion(bf16[2880,512]{1,0:T(8,128)(2,1)} %reshape.279, bf16[1024,512]{0,1:T(8,128)(2,1)} %bitcast.15), kind=kOutput, calls=%fused_computation.25 | convolution fusion | flops 3022848000 | bytes 9895936 | tf_op jit(solution)/shard_map/dot_general | solution.py:120
  219.1 8.5 %copy.88 = bf16[1024,2880]{1,0:T(8,128)(2,1)} copy(bf16[1024,2880]{0,1:T(8,128)(2,1)} %convolution_convert_fusion) | data formatting | bytes 11796480
  229.3 38.8 %reduce-scatter.4.cloned.1.call-done = bf16[128,2880]{1,0:T(8,128)(2,1)} async-done(((bf16[1024,2880]{1,0:T(8,128)(2,1)}), bf16[128,2880]{1,0:T(8,128)(2,1)}) %reduce-scatter.4.cloned.1.call-update) | async-done | bytes 737296 | tf_op jit(solution)/shard_map/reduce_scatter | solution.py:119
  269.6 4.7 convolution_convert_fusion.1
  274.2 6.6 %copy.81 = bf16[768,2880]{1,0:T(8,128)(2,1)} copy(bf16[768,2880]{0,1:T(8,128)(2,1)} %convolution_convert_fusion.1) | data formatting | bytes 8847360 | tf_op jit(solution)/shard_map/convert_element_type | solution.py:144
  280.8 7.6 %reshape.260 = bf16[128,6,2880]{2,1,0:T(8,128)(2,1)} reshape(bf16[768,2880]{1,0:T(8,128)(2,1)} %copy.81) | data formatting | bytes 8847360 | tf_op jit(solution)/shard_map/reshape | solution.py:145
  288.4 81.6 %all_to_all.10 = bf16[128,6,2880]{2,1,0:T(8,128)(2,1)} all-to-all(bf16[128,6,2880]{2,1,0:T(8,128)(2,1)} %reshape.260), channel_id=1, replica_groups=mesh['dp'=16,'tensor'=8] {'dp','tensor'}, dimensions={0} | all-to-all | bytes 8847360 | tf_op jit(solution)/shard_map/all_to_all | solution.py:149
  370.0 8.2 %reshape.261 = bf16[768,2880]{1,0:T(8,128)(2,1)} reshape(bf16[128,6,2880]{2,1,0:T(8,128)(2,1)} %all_to_all.10) | data formatting | bytes 8847360 | tf_op jit(solution)/shard_map/reshape | solution.py:33
  378.2 21.5 %fusion.16 = f32[768,2880]{0,1:T(8,128)} fusion(bf16[768,2880]{1,0:T(8,128)(2,1)} %reshape.261, bf16[1,2880,2880]{2,1,0:T(8,128)(2,1)} %param.26), kind=kOutput, calls=%fused_computation.20 | convolution fusion | flops 12740198400 | bytes 29859840 | tf_op jit(solution)/shard_map/dot_general | solution.py:34
  399.7 13.6 %fusion.20 = bf16[768,2880]{0,1:T(8,128)(2,1)} fusion(bf16[1,1440,2880]{2,1,0:T(8,128)(2,1)S(1)} %bitcast.74, f32[768,2880]{0,1:T(8,128)} %fusion.16), kind=kOutput, calls=%fused_computation.27 | convolution fusion | flops 6381158400 | bytes 21565440 | tf_op jit(solution)/shard_map/dot_general | solution.py:39
  413.3 6.5 %copy.82 = bf16[768,2880]{1,0:T(8,128)(2,1)} copy(bf16[768,2880]{0,1:T(8,128)(2,1)} %fusion.20) | data formatting | bytes 8847360 | tf_op jit(solution)/shard_map/convert_element_type | solution.py:39
  419.8 7.6 %reshape.262 = bf16[128,6,2880]{2,1,0:T(8,128)(2,1)} reshape(bf16[768,2880]{1,0:T(8,128)(2,1)} %copy.82) | data formatting | bytes 8847360 | tf_op jit(solution)/shard_map/reshape | solution.py:40
  427.4 6.6 %all-to-all-start.1 = ((bf16[128,6,2880]{2,1,0:T(8,128)(2,1)}), bf16[128,6,2880]{2,1,0:T(8,128)(2,1)}, u32[]{:S(2)}, u32[]{:S(2)}) async-start(bf16[128,6,2880]{2,1,0:T(8,128)(2,1)} %reshape.262), calls=%async_computation.1 | async-start | bytes 12058624 | tf_op jit(solution)/shard_map/all_to_all | solution.py:153
  434.5 72.2 %all-to-all-done.1 = bf16[128,6,2880]{2,1,0:T(8,128)(2,1)} async-done(((bf16[128,6,2880]{2,1,0:T(8,128)(2,1)}), bf16[128,6,2880]{2,1,0:T(8,128)(2,1)}, u32[]{:S(2)}, u32[]{:S(2)}) %all-to-all-start.1) | async-done | bytes 4423712 | tf_op jit(solution)/shard_map/all_to_all | solution.py:153
  506.7 8.2 %reshape.263 = bf16[768,2880]{1,0:T(8,128)(2,1)} reshape(bf16[128,6,2880]{2,1,0:T(8,128)(2,1)} %all-to-all-done.1) | data formatting | bytes 8847360 | tf_op jit(solution)/shard_map/reshape | solution.py:154
  514.9 9.6 %gather_fusion = bf16[512,2880]{1,0:T(8,128)(2,1)} fusion(bf16[768,2880]{1,0:T(8,128)(2,1)} %reshape.263, s32[1024]{0:T(1024)S(1)} %pad_clamp_fusion), kind=kCustom, calls=%fused_computation | custom fusion | bytes 5900288 | tf_op jit(solution)/shard_map/jit(_take)/gather | solution.py:155
  524.5 5.9 %gather.7 = bf16[128,4,2880]{2,1,0:T(4,128)(2,1)} reshape(bf16[512,2880]{1,0:T(8,128)(2,1)} %gather_fusion) | data formatting | bytes 5898240 | tf_op jit(solution)/shard_map/jit(_take)/gather | solution.py:155
  530.4 8.5 %multiply_reduce_fusion = f32[128,2880]{1,0:T(8,128)S(1)} fusion(f32[128,4]{1,0:T(8,128)S(1)} %copy.84, bf16[128,4,2880]{2,1,0:T(4,128)(2,1)} %gather.7, pred[128,4]{1,0:T(8,128)(4,1)S(1)} %copy.80), kind=kLoop, calls=%fused_computation.24 | loop fusion | flops 5529600 | bytes 4426240 | tf_op jit(solution)/shard_map/reduce_sum | solution.py:157
  (89 shorter events, 21.9 us)
Async XLA Ops:
  6.5 5.2 copy-start.7
  6.5 28.2 %copy-start.8 = (bf16[180,64]{0,1:T(8,128)(2,1)S(1)}, bf16[180,64]{0,1:T(8,128)(2,1)}, u32[]{:S(2)}) copy-start(bf16[180,64]{0,1:T(8,128)(2,1)} %param.20) | copy-start | bytes 69124
  6.5 55.2 %all-gather.10.cloned.1.call-start = ((), (), s32[]{:S(2)}) async-start(), calls=%async_computation.4 | async-start | bytes 3203072 | tf_op jit(solution)/shard_map/all_gather | solution.py:61
  7.3 103.1 %all-gather.12.cloned.1.call-start = ((), (), s32[]{:S(2)}) async-start(), calls=%async_computation.5 | async-start | bytes 3203072 | tf_op jit(solution)/shard_map/all_gather | solution.py:64
  8.0 143.5 %all-gather.8.cloned.1.call-start = ((), (), s32[]{:S(2)}) async-start(), calls=%async_computation.3 | async-start | bytes 6782976 | tf_op jit(solution)/shard_map/all_gather | solution.py:68
  9.8 46.3 %copy-start.12 = (s32[1,1024]{1,0:T(1,128)S(1)}, s32[1,1024]{1,0:T(1,128)}, u32[]{:S(2)}) copy-start(s32[1,1024]{1,0:T(1,128)} %param.16) | copy-start | bytes 12292
  11.6 256.5 %reduce-scatter.4.cloned.1.call-start = ((), (), s32[]{:S(2)}) async-start(), calls=%async_computation.6 | async-start | bytes 6782976 | tf_op jit(solution)/shard_map/reduce_scatter | solution.py:119
  66.1 85.4 %copy-start.3 = (bf16[2880,64]{1,0:T(8,128)(2,1)S(1)}, bf16[2880,64]{1,0:T(8,128)(2,1)}, u32[]{:S(2)}) copy-start(bf16[2880,64]{1,0:T(8,128)(2,1)} %reshape.281) | copy-start | bytes 1105924
  163.3 2.6 copy-start.2
  163.3 4.9 copy-start.1
  172.8 1.2 copy-start.4
  172.8 1.2 copy-start.5
  172.8 1.2 copy-start.6
  227.6 0.7 copy-start.9
  227.6 41.9 %copy-start.10 = (f32[2880]{0:T(1024)S(1)}, f32[2880]{0:T(1024)}, u32[]{:S(2)}) copy-start(f32[2880]{0:T(1024)} %param.23) | copy-start | bytes 34564
  370.0 29.7 %slice-start = ((s8[8478720]{0:T(1024)(128)(4,1)}), s8[90112]{0:T(1024)(128)(4,1)S(1)}, s32[]{:S(2)}) async-start(s8[8478720]{0:T(1024)(128)(4,1)} %bitcast.73), calls=%async_computation.7 | async-start | bytes 180224
  378.2 21.5 %slice-start.1 = ((s8[8478720]{0:T(1024)(128)(4,1)}), s8[4194304]{0:T(1024)(128)(4,1)S(1)}, s32[]{:S(2)}) async-start(s8[8478720]{0:T(1024)(128)(4,1)} %bitcast.73), calls=%async_computation.8 | async-start | bytes 8388608
  378.2 21.5 %slice-start.2 = ((s8[8478720]{0:T(1024)(128)(4,1)}), s8[4194304]{0:T(1024)(128)(4,1)S(1)}, s32[]{:S(2)}) async-start(s8[8478720]{0:T(1024)(128)(4,1)} %bitcast.73), calls=%async_computation.9 | async-start | bytes 8388608
  427.4 6.9 %copy-start.11 = (f32[128,4]{0,1:T(4,128)S(1)}, f32[128,4]{0,1:T(4,128)}, u32[]{:S(2)}) copy-start(f32[128,4]{0,1:T(4,128)} %param.25) | copy-start | bytes 6148
  427.4 79.3 %all-to-all-start.1 = ((bf16[128,6,2880]{2,1,0:T(8,128)(2,1)}), bf16[128,6,2880]{2,1,0:T(8,128)(2,1)}, u32[]{:S(2)}, u32[]{:S(2)}) async-start(bf16[128,6,2880]{2,1,0:T(8,128)(2,1)} %reshape.262), calls=%async_computation.1 | async-start | bytes 12058624 | tf_op jit(solution)/shard_map/all_to_all | solution.py:153
  524.5 14.4 %copy-start = (bf16[128,2880]{1,0:T(8,128)(2,1)S(1)}, bf16[128,2880]{1,0:T(8,128)(2,1)}, u32[]{:S(2)}) copy-start(bf16[128,2880]{1,0:T(8,128)(2,1)} %reduce-scatter.4.cloned.1.call-done) | copy-start | bytes 2211844
Sparse Core Ops, SparseCore 0:
  9.5 52.1 all-gather.9
  64.0 46.3 all-gather.11
  112.1 39.3 all-gather.7
  227.8 40.2 reduce-scatter.3
where the time goes:
time: 558 us; the launch traced here: 547 us
  waiting for transfers between devices  196 us (35%)
  blocking collectives  124 us (22%)
  local copies, waits for them, and re-layouts  91.8 us (16%)
  matrix products  77.9 us (14%)
  other arithmetic  36.5 us (7%)
  between operations  13.6 us (2%)
  starting transfers between devices  6.68 us (1%)
    all_to_all x1, blocking collectives, body(): lax.all_to_all(outgoing, ('dp', 'tensor'), split_axis=0, concat_axis=0, t...  81.6 us
    all_to_all x1, waiting for transfers between devices, body(): lax.all_to_all(finished, ('dp', 'tensor'), split_axis=0, concat_axis=0, t...  72.2 us
    all_gather x1, waiting for transfers between devices, body(): lax.all_gather(w_out, 'dp', axis=1, tiled=True)  44.3 us
    reduce_scatter x1, waiting for transfers between devices, body(): lax.psum_scatter(jnp.dot(heads, full_out, preferred_element_type=jnp.floa...  38.8 us
    all_gather x1, waiting for transfers between devices, body(): lax.all_gather(normed, 'tensor', axis=0, tiled=True)  36.8 us
    unnamed x45, local copies, waits for them, and re-layouts  28.6 us
    all_gather x1, blocking collectives, body(): lax.all_gather(key_weight, 'dp', axis=0, tiled=True)  22.4 us
    dot_general x1, matrix products, expert_apply(): both = jnp.dot(token_rows, gate_up, preferred_element_type=jnp.float32)  21.5 us
  transfers between devices with their start and end apart: 5, of which 5 were waited for; matrix products, arithmetic and copies ran while one was open for 3% of the time, Pallas kernels for 0%

commit v1 on v0

v1 whole, which is shorter than its diff:
```python
import math

import jax
import jax.numpy as jnp
from jax import lax
from jax.experimental import pallas as pl
from jax.experimental.pallas import tpu as pltpu
from jax.sharding import PartitionSpec as P

HEAD = 64
WIDTH = 2880
FF = 1440
CAP = 6
SLOTS = 8
MAIN = 2304
TAIL = WIDTH - MAIN
STEP = 640
BF = jnp.bfloat16
F32 = jnp.float32
NT = (((1,), (1,)), ((), ()))
TN = (((0,), (0,)), ((), ()))
VMEM = pl.BlockSpec(memory_space=pltpu.VMEM)
ANY = pl.BlockSpec(memory_space=pl.ANY)


def rms_norm(value_rows, gain):
    mean_square = jnp.mean(value_rows * value_rows, axis=-1, keepdims=True)
    return value_rows * lax.rsqrt(mean_square + 1e-05) * gain


def attend_kernel(x_ref, w_ref, cos_ref, sin_ref, docq_ref, dock_ref, out_ref, q_buf, k_buf, v_buf):
    block = pl.program_id(0)
    rows = x_ref.shape[0]
    length = k_buf.shape[0] // 2
    base = pl.multiple_of(block * rows, rows)
    here = pl.ds(base, rows)

    projected = jnp.dot(x_ref[...], w_ref[...], preferred_element_type=F32)
    lanes = lax.broadcasted_iota(jnp.int32, (rows, 128), 1)
    low = (lanes % HEAD) < HEAD // 2
    cosine = cos_ref[...]
    sine = sin_ref[...]

    def turn(pair):
        swapped = jnp.where(
            low, pltpu.roll(pair, 128 - HEAD // 2, 1), pltpu.roll(pair, HEAD // 2, 1)
        )
        return pair * cosine + swapped * sine

    pairs = out_ref.shape[1] // 128
    for pair in range(pairs):
        cols = slice(pair * 128, pair * 128 + 128)
        q_buf[:, cols] = (turn(projected[:, cols]) * HEAD ** (-0.5)).astype(BF)
    key_value = projected[:, pairs * 128 :]
    turned = turn(key_value)
    first = lanes < HEAD
    crossed = pltpu.roll(key_value, HEAD, 1)
    turned_crossed = pltpu.roll(turned, HEAD, 1)
    one = jnp.ones((rows, 128), F32)
    zero = jnp.zeros((rows, 128), F32)
    k_buf[here, :] = jnp.where(first, turned, 0.0).astype(BF)
    k_buf[pl.ds(length + base, rows), :] = jnp.where(first, 0.0, turned_crossed).astype(BF)
    v_buf[here, 0:128] = jnp.where(first, crossed, zero).astype(BF)
    v_buf[here, 128:256] = jnp.where(first, one, zero).astype(BF)
    v_buf[pl.ds(length + base, rows), 0:128] = jnp.where(first, zero, key_value).astype(BF)
    v_buf[pl.ds(length + base, rows), 128:256] = jnp.where(first, zero, one).astype(BF)

    def attend(blocks):
        span = blocks * rows
        start = pl.multiple_of(base + rows - span, rows)
        window = pl.ds(start, span)
        other = pl.ds(length + start, span)
        docs = dock_ref[:, pl.ds(start, span)]
        row = lax.broadcasted_iota(jnp.int32, (rows, span), 0) + (span - rows)
        col = lax.broadcasted_iota(jnp.int32, (rows, span), 1)
        allowed = (row >= col) & (docq_ref[...] == docs)
        key_a, key_b = k_buf[window, :], k_buf[other, :]
        value_a, value_b = v_buf[window, :], v_buf[other, :]
        for pair in range(pairs):
            cols = slice(pair * 128, pair * 128 + 128)
            query = q_buf[:, cols]
            both = None
            for keys, values in ((key_a, value_a), (key_b, value_b)):
                scores = lax.dot_general(query, keys, NT, preferred_element_type=F32)
                scores = jnp.where(allowed, scores, -1e30)
                largest = jnp.max(scores, axis=-1, keepdims=True)
                weights = jnp.exp(scores - largest).astype(BF)
                part = jnp.dot(weights, values, preferred_element_type=F32)
                both = part if both is None else both + part
            out_ref[:, cols] = (both[:, :128] / both[:, 128:]).astype(BF)

    for blocks in range(1, 5):
        pl.when(block == blocks - 1)(lambda blocks=blocks: attend(blocks))
    pl.when(block >= 4)(lambda: attend(5))


def attend(x, w, cosine, sine, docs):
    length, width = x.shape
    columns = w.shape[1] - 2 * HEAD
    rows = 128
    return pl.pallas_call(
        attend_kernel,
        out_shape=jax.ShapeDtypeStruct((length, columns), BF),
        grid=(length // rows,),
        in_specs=[
            pl.BlockSpec((rows, width), lambda i: (i, 0)),
            pl.BlockSpec((width, w.shape[1]), lambda i: (0, 0)),
            pl.BlockSpec((rows, 128), lambda i: (i, 0)),
            pl.BlockSpec((rows, 128), lambda i: (i, 0)),
            pl.BlockSpec((rows, 1), lambda i: (i, 0)),
            pl.BlockSpec((1, length), lambda i: (0, 0)),
        ],
        out_specs=pl.BlockSpec((rows, columns), lambda i: (i, 0)),
        scratch_shapes=[
            pltpu.VMEM((rows, columns), BF),
            pltpu.VMEM((2 * length, 128), BF),
            pltpu.VMEM((2 * length, 256), BF),
        ],
        compiler_params=pltpu.CompilerParams(vmem_limit_bytes=32 << 20),
        cost_estimate=pl.CostEstimate(
            flops=2 * length * width * w.shape[1] + 4 * length * 640 * columns * 2,
            bytes_accessed=2 * (length * width + width * w.shape[1] + length * columns),
            transcendentals=length * 640 * columns // HEAD,
        ),
        name="attend",
    )(x, w, cosine, sine, docs.reshape(length, 1), docs.reshape(1, length))


def dispatch_kernel(tokens_ref, attn_ref, gain_ref, table_ref, out_ref, resid_ref):
    rows = tokens_ref.shape[0]
    resid = tokens_ref[...].astype(F32) + attn_ref[...].astype(F32)
    resid_ref[...] = resid
    moe_in = rms_norm(resid, gain_ref[...]).astype(BF)
    tail = jnp.concatenate([moe_in[:, MAIN:], jnp.zeros((rows, STEP - TAIL), BF)], axis=1)
    top = table_ref[:, :rows]
    for j in range(3):
        cols = slice(j * STEP, (j + 1) * STEP)
        table = jnp.concatenate([top, table_ref[:, (j + 1) * rows : (j + 2) * rows]], axis=1)
        source = jnp.concatenate([moe_in[:, cols], tail], axis=0)
        out_ref[:, cols] = jnp.dot(table, source, preferred_element_type=F32).astype(BF)
    out_ref[:, 3 * STEP :] = jnp.dot(
        top, moe_in[:, 3 * STEP : MAIN], preferred_element_type=F32
    ).astype(BF)


def dispatch(tokens, attn_out, gain, table):
    rows, width = tokens.shape
    return pl.pallas_call(
        dispatch_kernel,
        out_shape=(
            jax.ShapeDtypeStruct((table.shape[0], MAIN), BF),
            jax.ShapeDtypeStruct((rows, width), F32),
        ),
        in_specs=[VMEM] * 4,
        out_specs=(VMEM, VMEM),
        compiler_params=pltpu.CompilerParams(vmem_limit_bytes=32 << 20),
        cost_estimate=pl.CostEstimate(
            flops=2 * table.shape[0] * 256 * MAIN,
            bytes_accessed=2 * table.shape[0] * (MAIN + 512) + 8 * rows * width,
            transcendentals=0,
        ),
        name="dispatch",
    )(tokens, attn_out, gain.reshape(1, width), table)


def expert_kernel(
    recv_ref, gate_up_ref, down_ref, pick_ref, put_ref, out_ref,
    x_buf, gate_up_buf, down_buf, both_buf, act_buf, y_buf, sems,
):
    total = x_buf.shape[0]
    tiles = [(s, min(512, WIDTH - s)) for s in range(0, WIDTH, 512)]
    copies = []
    for i, (start, size) in enumerate(tiles):
        cols = pl.ds(start, size)
        copies.append(
            pltpu.make_async_copy(gate_up_ref.at[:, cols], gate_up_buf.at[:, cols], sems.at[i])
        )
    down_copy = pltpu.make_async_copy(down_ref, down_buf, sems.at[len(tiles)])
    for copy in copies:
        copy.start()
    down_copy.start()

    blocks = recv_ref.shape[0] // 128
    packed = 128 // SLOTS * CAP

    def unpack(block, carry):
        source = pl.ds(pl.multiple_of(block * 128, 128), 128)
        target = pl.ds(pl.multiple_of(block * packed, packed), packed)
        tail = jnp.zeros((packed, STEP), F32)
        for j in range(3):
            cols = slice(j * STEP, (j + 1) * STEP)
            pair = jnp.dot(pick_ref[j], recv_ref[source, cols], preferred_element_type=F32)
            x_buf[target, cols] = pair[:packed].astype(BF)
            tail = tail + pair[packed:]
        x_buf[target, 3 * STEP : MAIN] = jnp.dot(
            pick_ref[0, :packed], recv_ref[source, 3 * STEP : MAIN], preferred_element_type=F32
        ).astype(BF)
        x_buf[target, MAIN:] = tail[:, :TAIL].astype(BF)
        return carry

    lax.fori_loop(0, blocks, unpack, 0)

    chunk = total // 3
    for i, (start, size) in enumerate(tiles):
        copies[i].wait()

        def multiply(m, carry, start=start, size=size):
            rows = pl.ds(pl.multiple_of(m * chunk, chunk), chunk)
            both_buf[rows, start : start + size] = jnp.dot(
                x_buf[rows, :], gate_up_buf[:, start : start + size], preferred_element_type=F32
            )
            return carry

        lax.fori_loop(0, 3, multiply, 0)

    def activate(m, carry):
        rows = pl.ds(pl.multiple_of(m * 64, 64), 64)
        gate = both_buf[rows, :FF]
        up = both_buf[rows, FF:]
        act_buf[rows, :] = (gate * jax.nn.sigmoid(1.702 * gate) * (up + 1.0)).astype(BF)
        return carry

    lax.fori_loop(0, total // 64, activate, 0)

    down_copy.wait()
    for start, size in tiles:

        def multiply_down(m, carry, start=start, size=size):
            rows = pl.ds(pl.multiple_of(m * chunk, chunk), chunk)
            y_buf[rows, start : start + size] = jnp.dot(
                act_buf[rows, :], down_buf[:, start : start + size], preferred_element_type=F32
            ).astype(BF)
            return carry

        lax.fori_loop(0, 3, multiply_down, 0)

    def pack(block, carry):
        target = pl.ds(pl.multiple_of(block * 128, 128), 128)
        source = pl.ds(pl.multiple_of(block * packed, packed), packed)
        tail = jnp.concatenate(
            [y_buf[source, MAIN:], jnp.zeros((packed, STEP - TAIL), BF)], axis=1
        )
        for j in range(3):
            cols = slice(j * STEP, (j + 1) * STEP)
            pair = jnp.concatenate([y_buf[source, cols], tail], axis=0)
            out_ref[target, cols] = jnp.dot(
                put_ref[j], pair, preferred_element_type=F32
            ).astype(BF)
        out_ref[target, 3 * STEP :] = jnp.dot(
            put_ref[0, :, :packed], y_buf[source, 3 * STEP : MAIN], preferred_element_type=F32
        ).astype(BF)
        return carry

    lax.fori_loop(0, blocks, pack, 0)


def experts(recv, gate_up, down):
    packed = 128 // SLOTS * CAP
    row = jnp.arange(packed, dtype=jnp.int32)
    source, slot = row // CAP, row % CAP
    col = jnp.arange(128, dtype=jnp.int32)[None, :]
    main = (col == (source * SLOTS + slot)[:, None]).astype(BF)
    place = (source * SLOTS + CAP + slot // 3)[:, None]
    pick = jnp.stack(
        [
            jnp.concatenate([main, ((col == place) & (slot % 3 == j)[:, None]).astype(BF)], axis=0)
            for j in range(3)
        ]
    )
    put = pick.transpose(0, 2, 1)
    total = recv.shape[0] // SLOTS * CAP
    return pl.pallas_call(
        expert_kernel,
        out_shape=jax.ShapeDtypeStruct(recv.shape, BF),
        in_specs=[VMEM, ANY, ANY, VMEM, VMEM],
        out_specs=VMEM,
        scratch_shapes=[
            pltpu.VMEM((total, WIDTH), BF),
            pltpu.VMEM((WIDTH, 2 * FF), BF),
            pltpu.VMEM((FF, WIDTH), BF),
            pltpu.VMEM((total, 2 * FF), F32),
            pltpu.VMEM((total, FF), BF),
            pltpu.VMEM((total, WIDTH), BF),
            pltpu.SemaphoreType.DMA((7,)),
        ],
        compiler_params=pltpu.CompilerParams(vmem_limit_bytes=60 << 20),
        cost_estimate=pl.CostEstimate(
            flops=6 * total * FF * WIDTH,
            bytes_accessed=6 * FF * WIDTH + 4 * recv.shape[0] * MAIN,
            transcendentals=total * FF,
        ),
        name="experts",
    )(recv, gate_up, down, pick, put)


def combine_kernel(back_ref, resid_ref, coef_ref, out_ref):
    rows = resid_ref.shape[0]
    wide = 2 * rows
    main = lax.dot_general(coef_ref[:, :wide], back_ref[...], TN, preferred_element_type=F32)
    out_ref[:, :MAIN] = (resid_ref[:, :MAIN] + (main[:rows] + main[rows:])).astype(BF)
    tail = jnp.zeros((rows, STEP), F32)
    for j in range(3):
        part = lax.dot_general(
            coef_ref[:, (j + 1) * wide : (j + 2) * wide],
            back_ref[:, j * STEP : (j + 1) * STEP],
            TN,
            preferred_element_type=F32,
        )
        tail = tail + (part[:rows] + part[rows:])
    out_ref[:, MAIN:] = (resid_ref[:, MAIN:] + tail[:, :TAIL]).astype(BF)


def combine(back, resid, coef):
    rows, width = resid.shape
    return pl.pallas_call(
        combine_kernel,
        out_shape=jax.ShapeDtypeStruct((rows, width), BF),
        in_specs=[VMEM] * 3,
        out_specs=VMEM,
        compiler_params=pltpu.CompilerParams(vmem_limit_bytes=32 << 20),
        cost_estimate=pl.CostEstimate(
            flops=4 * back.shape[0] * rows * (MAIN + 3 * STEP),
            bytes_accessed=2 * back.shape[0] * (MAIN + 1024) + 6 * rows * width,
            transcendentals=0,
        ),
        name="combine",
    )(back, resid, coef)


def routing(expert_ids, gate_weights, experts_count):
    rows = expert_ids.shape[0]
    names = jnp.arange(experts_count, dtype=jnp.int32)
    named = expert_ids.T[:, None, :] == names[None, :, None]
    hit = jnp.any(named, axis=0)
    share = gate_weights / jnp.sum(gate_weights, axis=-1, keepdims=True)
    weight = jnp.sum(jnp.where(named, share.T[:, None, :], 0.0), axis=0)
    index = jnp.arange(rows, dtype=jnp.int32)
    earlier = (index[:, None] < index[None, :]).astype(BF)
    rank = jnp.dot(hit.astype(BF), earlier, preferred_element_type=F32).astype(jnp.int32)
    rank = jnp.where(hit, rank, -1)[:, None, :]
    slot = jnp.arange(SLOTS, dtype=jnp.int32)[None, :, None]
    layers = [(rank == slot) & (slot < CAP)]
    for j in range(3):
        layers.append(
            ((slot == CAP) & (rank == j)) | ((slot == CAP + 1) & (rank == j + 3))
        )
    flat = [layer.reshape(experts_count * SLOTS, rows) for layer in layers]
    table = jnp.concatenate([layer.astype(BF) for layer in flat], axis=1)
    spread = jnp.broadcast_to(
        weight[:, None, :], (experts_count, SLOTS, rows)
    ).reshape(experts_count * SLOTS, rows)
    high = spread.astype(BF)
    low = (spread - high.astype(F32)).astype(BF)
    none = jnp.zeros((), BF)
    coef = jnp.concatenate(
        [jnp.where(layer, part, none) for layer in flat for part in (high, low)], axis=1
    )
    return table, coef


def body(
    tokens,
    positions,
    doc_ids,
    w_query,
    key_weight,
    value_weight,
    w_out,
    attn_gain,
    moe_gain,
    expert_ids,
    gate_weights,
    w_gate_up,
    w_down,
):
    normed = rms_norm(tokens.astype(F32), attn_gain).astype(BF)
    joined = jnp.concatenate([w_query, key_weight, value_weight], axis=1)
    full_joined = lax.all_gather(joined, "dp", axis=0, tiled=False).reshape(-1, joined.shape[1])
    window = lax.all_gather(normed, "tensor", axis=0, tiled=True)
    full_out = lax.all_gather(w_out, "dp", axis=1, tiled=True)

    half = HEAD // 2
    freq = jnp.exp(jnp.arange(half, dtype=F32) * (-2.0 * math.log(150000.0) / HEAD))
    angle = positions[0].astype(F32)[:, None] * freq[None, :]
    cosine, sine = jnp.cos(angle), jnp.sin(angle)
    cosine = jnp.concatenate([cosine] * 4, axis=1)
    sine = jnp.concatenate([-sine, sine] * 2, axis=1)
    experts_count = lax.axis_size("dp") * lax.axis_size("tensor")
    table, coef = routing(expert_ids, gate_weights, experts_count)

    heads = attend(window, full_joined, cosine, sine, doc_ids[0])
    partial_sums = jnp.dot(heads, full_out, preferred_element_type=F32).astype(BF)
    attn_out = lax.psum_scatter(partial_sums, "tensor", scatter_dimension=0, tiled=True)
    outgoing, resid = dispatch(tokens, attn_out, moe_gain, table)
    received = lax.all_to_all(outgoing, ("dp", "tensor"), split_axis=0, concat_axis=0, tiled=True)
    finished = experts(received, w_gate_up[0], w_down[0])
    returned = lax.all_to_all(finished, ("dp", "tensor"), split_axis=0, concat_axis=0, tiled=True)
    return combine(returned, resid, coef)


def solution(mesh):
    placed = (
        P(("dp", "tensor"), None),
        P("dp", None),
        P("dp", None),
        P("dp", "tensor"),
        P("dp", "tensor"),
        P("dp", "tensor"),
        P("tensor", "dp"),
        P(),
        P(),
        P(("dp", "tensor"), None),
        P(("dp", "tensor"), None),
        P(("dp", "tensor"), None, None),
        P(("dp", "tensor"), None, None),
    )
    return jax.shard_map(
        body, mesh=mesh, in_specs=placed, out_specs=P(("dp", "tensor"), None), check_vma=False
    )
```

time: 558 us -> 424 us (0.76); the launches traced: 547 us -> 423 us
  blocking collectives: 124 us -> 0 us
  waiting for transfers between devices: 196 us -> 274 us
  matrix products: 77.9 us -> 5.24 us
  Pallas kernels: 0 us -> 64.6 us
  local copies, waits for them, and re-layouts: 91.8 us -> 34.7 us
  other arithmetic: 36.5 us -> 14.4 us
  starting transfers between devices: 6.68 us -> 16.2 us
    all_to_all x1 -> x0, blocking collectives: 81.6 us -> none  [body(): lax.all_to_all(outgoing, ('dp', 'tensor'), split_axis=0, concat_axis=0, t...]
    dot_general x22 -> x2, matrix products: 77.9 us -> 5.24 us  [the longest x1 5.04 us: body(): jnp.dot(heads, full_out, preferred_element_type=F32).astype(BF)]
    pallas_call x0 -> x4, Pallas kernels: none -> 64.6 us  [the longest x1 40.2 us: experts(): pl.pallas_call(expert_kernel, out_shape=jax.ShapeDtypeStruct(recv.shape,...]
    all_to_all x0 -> x1, waiting for transfers between devices: none -> 56.8 us  [body(): lax.all_to_all(outgoing, ('dp', 'tensor'), split_axis=0, concat_axis=0, t...]
    all_gather x3, waiting for transfers between devices: 83.8 us -> 127 us  [the longest x1 46.9 us: body(): lax.all_gather(joined, 'dp', axis=0, tiled=False)]
    all_gather x2 -> x0, blocking collectives: 42.2 us -> none  [the longest x1 22.4 us: body(): lax.all_gather(key_weight, 'dp', axis=0, tiled=True)]
    reshape x6 -> x1, local copies, waits for them, and re-layouts: 32.4 us -> 0.01 us  [dispatch(): gain.reshape(1, width)]
    reduce_sum x10 -> x2, other arithmetic: 23.2 us -> 0.05 us  [the longest x1 0.03 us: routing(): weight = jnp.sum(jnp.where(named, share.T[:, None, :], 0.0), axis=0)]
  transfers between devices with their start and end apart: 5 -> 6, of which waited for: 5 -> 6; matrix products, arithmetic and copies ran while one was open for 3% -> 7% of each run, Pallas kernels for 0% -> 0%
where the time goes in v1:
time: 424 us; the launch traced here: 423 us
  waiting for transfers between devices  274 us (65%)
  Pallas kernels  64.6 us (15%)
  local copies, waits for them, and re-layouts  34.7 us (8%)
  starting transfers between devices  16.2 us (4%)
  other arithmetic  14.4 us (3%)
  between operations  13.5 us (3%)
  matrix products  5.24 us (1%)
    all_to_all x1, waiting for transfers between devices, body(): lax.all_to_all(outgoing, ('dp', 'tensor'), split_axis=0, concat_axis=0, t...  56.8 us
    all_to_all x1, waiting for transfers between devices, body(): lax.all_to_all(finished, ('dp', 'tensor'), split_axis=0, concat_axis=0, t...  52.4 us
    all_gather x1, waiting for transfers between devices, body(): lax.all_gather(joined, 'dp', axis=0, tiled=False)  46.9 us
    all_gather x1, waiting for transfers between devices, body(): full_out = lax.all_gather(w_out, 'dp', axis=1, tiled=True)  43.3 us
    pallas_call x1, Pallas kernels, experts(): pl.pallas_call(expert_kernel, out_shape=jax.ShapeDtypeStruct(recv.shape,...  40.2 us
    reduce_scatter x1, waiting for transfers between devices, body(): lax.psum_scatter(partial_sums, 'tensor', scatter_dimension=0, tiled=True)  37.5 us
    all_gather x1, waiting for transfers between devices, body(): window = lax.all_gather(normed, 'tensor', axis=0, tiled=True)  36.7 us
    unnamed x31, local copies, waits for them, and re-layouts  23.6 us
  transfers between devices with their start and end apart: 6, of which 6 were waited for; matrix products, arithmetic and copies ran while one was open for 7% of the time, Pallas kernels for 0%

profile of v1, /device:TPU:1, one launch (start us, length us, event | category | flops | bytes accessed | tf_op | source)
XLA Modules:
  0.0 422.9 jit_solution(15410287144574630622)
XLA Ops:
  6.5 0.7 all-gather.11.cloned.1.call-update
  7.3 0.9 copy.47
  8.2 0.9 copy.46
  9.0 1.7 maximum_bitcast_fusion
  10.9 1.5 copy.51.tokens_ref
  12.3 0.2 fusion
  12.6 1.1 fusion.2
  13.8 0.2 copy.49.docq_ref
  14.1 1.9 fusion.27
  16.0 0.9 pad_maximum_fusion
  16.9 43.3 %all-gather.11.cloned.1.call-done = bf16[16,180,512]{2,1,0:T(8,128)(2,1)} async-done(((bf16[1,180,512]{2,1,0:T(8,128)(2,1)}), bf16[16,180,512]{2,1,0:T(8,128)(2,1)}) %all-gather.11.cloned.1.call-update) | async-done | bytes 2949136 | tf_op jit(solution)/shard_map/all_gather | solution.py:380
  60.2 4.3 %reshape.136 = bf16[2880,512]{1,0:T(8,128)(2,1)} reshape(bf16[16,180,512]{2,1,0:T(8,128)(2,1)} %all-gather.11.cloned.1.call-done) | data formatting | bytes 5898240
  64.5 46.9 %all-gather.9.cloned.1.call-done = bf16[16,180,640]{2,1,0:T(8,128)(2,1)} async-done(((bf16[1,180,640]{2,1,0:T(8,128)(2,1)}), bf16[16,180,640]{2,1,0:T(8,128)(2,1)}) %all-gather.9.cloned.1.call-update) | async-done | bytes 3686416 | tf_op jit(solution)/shard_map/all_gather | solution.py:378
  111.4 4.8 %reshape.134.w_ref = bf16[2880,640]{1,0:T(8,128)(2,1)} reshape(bf16[16,180,640]{2,1,0:T(8,128)(2,1)} %all-gather.9.cloned.1.call-done) | data formatting | bytes 7372800
  116.1 36.7 %all-gather.7.cloned.1.call-done.x_ref = bf16[1024,2880]{1,0:T(8,128)(2,1)} async-done(((bf16[128,2880]{1,0:T(8,128)(2,1)}), bf16[1024,2880]{1,0:T(8,128)(2,1)}) %all-gather.7.cloned.1.call-update) | async-done | bytes 5898256 | tf_op jit(solution)/shard_map/all_gather | solution.py:379
  152.8 2.0 copy-done.1
  154.8 2.7 copy-done.5
  157.6 17.4 %attend.1 = bf16[1024,512]{1,0:T(8,128)(2,1)S(1)} custom-call(bf16[1024,2880]{1,0:T(8,128)(2,1)S(1)} %copy-done.5, bf16[2880,640]{1,0:T(8,128)(2,1)S(1)} %copy-done.1, f32[1024,128]{1,0:T(8,128)S(1)} %get-tuple-element.30.cos_ref, f32[1024,128]{1,0:T(8,128)S(1)} %get-tuple-element.31.sin_ref, s32[1024,1]{1,0:T(8,128)S(1)} %copy.49.docq_ref, ...), custom_call_target="tpu_custom_call" | custom-call | flops 6459228160 | bytes 10633216 | tf_op jit(solution)/shard_map/attend/pallas_call | solution.py:101
  175.0 5.0 %convolution_convert_fusion = bf16[1024,2880]{0,1:T(8,128)(2,1)} fusion(bf16[1024,512]{1,0:T(8,128)(2,1)S(1)} %attend.1, bf16[2880,512]{1,0:T(8,128)(2,1)S(1)} %copy-done.7), kind=kOutput, calls=%fused_computation | convolution fusion | flops 3022848000 | bytes 9895936 | tf_op jit(solution)/shard_map/dot_general | solution.py:392
  180.0 8.5 %copy.50 = bf16[1024,2880]{1,0:T(8,128)(2,1)} copy(bf16[1024,2880]{0,1:T(8,128)(2,1)} %convolution_convert_fusion) | data formatting | bytes 11796480 | tf_op jit(solution)/shard_map/convert_element_type | solution.py:392
  188.6 0.7 copy-done.9
  189.8 0.2 broadcast_compare_fusion.5
  190.0 0.3 fusion.14
  190.4 0.8 fusion.17
  191.2 0.3 add_convert_fusion.table_ref
  191.5 37.5 %reduce-scatter.2.cloned.1.call-done.attn_ref = bf16[128,2880]{1,0:T(8,128)(2,1)} async-done(((bf16[1024,2880]{1,0:T(8,128)(2,1)}), bf16[128,2880]{1,0:T(8,128)(2,1)}) %reduce-scatter.2.cloned.1.call-update) | async-done | bytes 737296 | tf_op jit(solution)/shard_map/reduce_scatter | solution.py:393
  229.0 1.1 copy-done.6
  230.1 2.0 dispatch.1
  232.1 2.2 copy-done
  234.3 1.1 copy-done.2
  235.4 9.2 %all-to-all-start = ((bf16[128,8,2304]{2,1,0:T(8,128)(2,1)}), bf16[128,8,2304]{2,1,0:T(8,128)(2,1)}, u32[]{:S(2)}, u32[]{:S(2)}) async-start(bf16[128,8,2304]{2,1,0:T(8,128)(2,1)} %bitcast.124), calls=%async_computation.1 | async-start | bytes 9437184 | tf_op jit(solution)/shard_map/all_to_all | solution.py:395
  245.0 0.7 fusion.42
  245.7 0.8 copy.52.pick_ref
  246.5 56.8 %all-to-all-done = bf16[128,8,2304]{2,1,0:T(8,128)(2,1)} async-done(((bf16[128,8,2304]{2,1,0:T(8,128)(2,1)}), bf16[128,8,2304]{2,1,0:T(8,128)(2,1)}, u32[]{:S(2)}, u32[]{:S(2)}) %all-to-all-start) | async-done | bytes 4718624 | tf_op jit(solution)/shard_map/all_to_all | solution.py:395
  303.2 40.2 %experts.1 = bf16[1024,2304]{1,0:T(8,128)(2,1)} custom-call(bf16[1024,2304]{1,0:T(8,128)(2,1)} %bitcast.14.recv_ref, bf16[2880,2880]{1,0:T(8,128)(2,1)} %bitcast.131, bf16[1440,2880]{1,0:T(8,128)(2,1)} %bitcast.132, bf16[3,192,128]{2,1,0:T(8,128)(2,1)} %copy.52.pick_ref, bf16[3,128,192]{2,1,0:T(8,128)(2,1)} %get-tuple-element.9.put_ref), custom_call_target="tpu_custom_call" | custom-call | flops 19110297600 | bytes 34320384 | tf_op jit(solution)/shard_map/experts/pallas_call | solution.py:272
  343.4 6.8 %all-to-all-start.1 = ((bf16[128,8,2304]{2,1,0:T(8,128)(2,1)}), bf16[128,8,2304]{2,1,0:T(8,128)(2,1)}, u32[]{:S(2)}, u32[]{:S(2)}) async-start(bf16[128,8,2304]{2,1,0:T(8,128)(2,1)} %bitcast.126), calls=%async_computation.2 | async-start | bytes 9437184 | tf_op jit(solution)/shard_map/all_to_all | solution.py:397
  350.4 0.3 fusion.22
  350.7 0.4 fusion.18
  351.1 0.9 fusion.23
  352.0 0.9 fusion.19
  352.9 0.9 fusion.24
  353.8 0.9 fusion.20
  354.7 0.9 fusion.25
  355.5 0.9 fusion.21.coef_ref
  356.4 52.4 %all-to-all-done.1 = bf16[128,8,2304]{2,1,0:T(8,128)(2,1)} async-done(((bf16[128,8,2304]{2,1,0:T(8,128)(2,1)}), bf16[128,8,2304]{2,1,0:T(8,128)(2,1)}, u32[]{:S(2)}, u32[]{:S(2)}) %all-to-all-start.1) | async-done | bytes 4718624 | tf_op jit(solution)/shard_map/all_to_all | solution.py:397
  408.8 1.4 copy-done.3
  410.2 5.0 %combine.1 = bf16[128,2880]{1,0:T(8,128)(2,1)S(1)} custom-call(bf16[1024,2304]{1,0:T(8,128)(2,1)} %bitcast.22.back_ref, f32[128,2880]{1,0:T(8,128)S(1)} %copy-done.3, bf16[1024,1024]{1,0:T(8,128)(2,1)S(1)} %fusion.21.coef_ref), custom_call_target="tpu_custom_call" | custom-call | flops 2214592512 | bytes 9027584 | tf_op jit(solution)/shard_map/combine/pallas_call | solution.py:315
  415.2 1.1 copy.53
  (52 shorter events, 1.0 us)
Async XLA Ops:
  6.5 6.0 %copy-start.8 = (f32[2880]{0:T(1024)S(1)}, f32[2880]{0:T(1024)}, u32[]{:S(2)}) copy-start(f32[2880]{0:T(1024)} %param.20) | copy-start | bytes 34564
  6.5 53.6 %all-gather.11.cloned.1.call-start = ((), (), s32[]{:S(2)}) async-start(), calls=%async_computation.6 | async-start | bytes 3203072 | tf_op jit(solution)/shard_map/all_gather | solution.py:380
  7.3 104.1 %all-gather.9.cloned.1.call-start = ((), (), s32[]{:S(2)}) async-start(), calls=%async_computation.5 | async-start | bytes 4003840 | tf_op jit(solution)/shard_map/all_gather | solution.py:378
  10.8 3.0 copy-start.12
  10.8 3.0 copy-start.4
  10.8 142.0 %all-gather.7.cloned.1.call-start = ((), (), s32[]{:S(2)}) async-start(), calls=%async_computation.3 | async-start | bytes 6782976 | tf_op jit(solution)/shard_map/all_gather | solution.py:379
  13.7 215.3 %reduce-scatter.2.cloned.1.call-start = ((), (), s32[]{:S(2)}) async-start(), calls=%async_computation.4 | async-start | bytes 6782976 | tf_op jit(solution)/shard_map/reduce_scatter | solution.py:393
  152.8 2.0 copy-start.1
  154.8 2.7 copy-start.5
  157.6 17.4 %copy-start.7 = (bf16[2880,512]{1,0:T(8,128)(2,1)S(1)}, bf16[2880,512]{1,0:T(8,128)(2,1)}, u32[]{:S(2)}) copy-start(bf16[2880,512]{1,0:T(8,128)(2,1)} %reshape.136) | copy-start | bytes 8847364
  188.6 0.7 copy-start.9
  188.6 1.2 copy-start.10
  229.0 1.1 copy-start.6
  232.1 2.2 copy-start
  234.3 1.1 copy-start.2
  235.4 67.8 %all-to-all-start = ((bf16[128,8,2304]{2,1,0:T(8,128)(2,1)}), bf16[128,8,2304]{2,1,0:T(8,128)(2,1)}, u32[]{:S(2)}, u32[]{:S(2)}) async-start(bf16[128,8,2304]{2,1,0:T(8,128)(2,1)} %bitcast.124), calls=%async_computation.1 | async-start | bytes 9437184 | tf_op jit(solution)/shard_map/all_to_all | solution.py:395
  343.4 6.9 %copy-start.11 = (f32[128,4]{0,1:T(4,128)S(1)}, f32[128,4]{0,1:T(4,128)}, u32[]{:S(2)}) copy-start(f32[128,4]{0,1:T(4,128)} %param.23) | copy-start | bytes 6148
  343.4 65.4 %all-to-all-start.1 = ((bf16[128,8,2304]{2,1,0:T(8,128)(2,1)}), bf16[128,8,2304]{2,1,0:T(8,128)(2,1)}, u32[]{:S(2)}, u32[]{:S(2)}) async-start(bf16[128,8,2304]{2,1,0:T(8,128)(2,1)} %bitcast.126), calls=%async_computation.2 | async-start | bytes 9437184 | tf_op jit(solution)/shard_map/all_to_all | solution.py:397
  408.8 1.4 copy-start.3
Sparse Core Ops, SparseCore 0:
  9.5 50.5 all-gather.10
  62.3 48.9 all-gather.8
  113.1 39.6 all-gather.6
  188.7 40.2 reduce-scatter.1
